TPU v7x, 32 devices: a whole 2x2x4 slice. The times are simulated.
32 devices in a mesh: space: 4 (over z), member: 4 (over y, x), lag: 2 (over core).
Axes of the slice: x: 2, y: 2, z: 4, core: 2. Of those that a mesh axis runs over, the one named last changes fastest.
Arguments:
- anomalies: bfloat16 [2, 16384, 512], P('lag', 'space', 'member'), may hold values from -6 to 6
- mean_state: float32 [2, 16384], P('lag', 'space'), may hold values from -6 to 6
- footprints: bfloat16 [4, 2, 16, 256, 512], P(None, 'lag', 'space'), may hold values from -0.09375 to 0.09375
- slot_tiles: int32 [4, 2, 16], P(None, 'lag', 'space'), may hold values from 0 to 7, as said below
- slot_counts: int32 [4, 2, 4], P(None, 'lag', 'space'), may hold values from 0 to 4, as said below
- obs_values: float32 [4, 4, 256], P('space'), may hold values from -6 to 6
- obs_errors: float32 [4, 4, 256], P('space'), may hold values from 0.5 to 1.5
- owners: int32 [4], replicated, may hold values from 0 to 3
- batch_order: int32 [4], replicated, may hold values from 0 to 3, as said below
Outputs:
- analysis_anoms: bfloat16 [2, 16384, 512], P('lag', 'space', 'member')
- analysis_mean: float32 [2, 16384], P('lag', 'space')
Inputs may be any that keep to these rules, and one draw needn't show every extreme that they name: `slot_counts`: in every batch some lag week and space group has exactly 4 live slots. `slot_tiles`: within one batch, lag week and space group the 4 slots name distinct local tiles. `batch_order`: A permutation.
All inputs are finite; a program needn't handle non-finite values.
Results may differ from a plain program's by a relative error of at most 0.008.
Values may be sent and summed in bfloat16 or wider, within the bound.
A program may use at most 64 MiB of HBM per device.

v0:
```python
import jax
import jax.numpy as jnp
from jax import lax
from jax.sharding import PartitionSpec as P


def innovation(obs_round, values_now, obs_means, errors_now, members):
    obs_total = obs_round.shape[0]
    innov_cov = jnp.dot(obs_round, obs_round.T, preferred_element_type=jnp.float32) / (
        members - 1
    ) + jnp.diag(errors_now * errors_now)
    factor = jnp.linalg.cholesky(innov_cov)
    identity = jnp.eye(obs_total, dtype=jnp.float32)
    inverse_sum = lax.linalg.triangular_solve(
        factor + jnp.diag(errors_now), identity, left_side=True, lower=True
    )
    transform = lax.linalg.triangular_solve(
        factor, inverse_sum, left_side=True, lower=True, transpose_a=True
    )
    forward = lax.linalg.triangular_solve(
        factor, (values_now - obs_means)[:, None], left_side=True, lower=True
    )
    weights_obs = lax.linalg.triangular_solve(
        factor, forward, left_side=True, lower=True, transpose_a=True
    )[:, 0]
    return (transform, weights_obs)


def body(
    anomalies,
    mean_state,
    footprints,
    slot_tiles,
    slot_counts,
    obs_values,
    obs_errors,
    owners,
    batch_order,
):
    highest = lax.Precision.HIGHEST
    batches = footprints.shape[0]
    slot_dev = footprints.shape[2]
    tile_cells = footprints.shape[4]
    member_dev = anomalies.shape[2]
    groups = lax.axis_size("member")
    members = member_dev * groups
    tile_anoms = anomalies[0].reshape(-1, tile_cells, member_dev)
    tile_means = mean_state[0].reshape(-1, tile_cells)
    owned_here = owners == lax.axis_index("space")
    own_values = jnp.where(owned_here[:, None], obs_values[0], 0.0)
    own_errors = jnp.where(owned_here[:, None], obs_errors[0], 0.0)
    all_values, all_errors = lax.psum((own_values, own_errors), "space")
    for position in range(batches):
        batch_now = batch_order[position]
        values_now = all_values[batch_now]
        errors_now = all_errors[batch_now]
        tile_ids = slot_tiles[batch_now, 0]
        live_count = slot_counts[batch_now, 0, 0]
        live_mask = jnp.arange(slot_dev) < live_count
        slot_anoms = tile_anoms[tile_ids]
        slot_means = tile_means[tile_ids]
        prints = footprints[batch_now, 0]
        mean_round = slot_means.astype(jnp.bfloat16)
        masked = jnp.where(live_mask[:, None, None], slot_anoms, 0)
        part_anoms = jnp.einsum("spt,stm->pm", prints, masked, preferred_element_type=jnp.float32)
        masked_mean = jnp.where(live_mask[:, None], mean_round, 0)
        part_means = jnp.einsum(
            "spt,st->p", prints, masked_mean, preferred_element_type=jnp.float32
        )
        obs_anoms, obs_means = lax.psum((part_anoms, part_means), ("space", "lag"))
        own_round = obs_anoms.astype(jnp.bfloat16)
        obs_round = lax.all_gather(own_round, "member", axis=1, tiled=True)
        transform, weights_obs = innovation(obs_round, values_now, obs_means, errors_now, members)
        all_anoms = lax.all_gather(slot_anoms, "member", axis=2, tiled=True)
        covariance = jnp.einsum(
            "stm,pm->stp", all_anoms, obs_round, preferred_element_type=jnp.float32
        )
        gain_tile = (
            jnp.einsum("stp,pq->stq", covariance, transform, precision=highest) / (members - 1)
        ).astype(jnp.bfloat16)
        shift_mean = jnp.einsum("stp,p->st", covariance, weights_obs, precision=highest) / (
            members - 1
        )
        step_anoms = jnp.einsum(
            "stp,pm->stm", gain_tile, own_round, preferred_element_type=jnp.float32
        )
        updated = (slot_anoms.astype(jnp.float32) - step_anoms).astype(jnp.bfloat16)
        tile_anoms = tile_anoms.at[tile_ids].set(
            jnp.where(live_mask[:, None, None], updated, slot_anoms)
        )
        tile_means = tile_means.at[tile_ids].set(
            jnp.where(live_mask[:, None], slot_means + shift_mean, slot_means)
        )
    return (tile_anoms.reshape(1, -1, member_dev), tile_means.reshape(1, -1))


def solution(mesh):
    return jax.shard_map(
        body,
        mesh=mesh,
        in_specs=(
            P("lag", "space", "member"),
            P("lag", "space"),
            P(None, "lag", "space", None, None),
            P(None, "lag", "space"),
            P(None, "lag", "space"),
            P("space", None, None),
            P("space", None, None),
            P(),
            P(),
        ),
        out_specs=(P("lag", "space", "member"), P("lag", "space")),
        check_vma=False,
    )
```

profile of v0, /device:TPU:0, one launch (start us, length us, event | category | flops | bytes accessed | tf_op | source)
XLA Modules:
  0.0 629.6 jit_solution(14047488163257396615)
XLA Ops:
  19.9 1.9 convolution_bitcast_fusion.3
  23.6 1.6 fusion.29
  25.2 32.1 %all-reduce.10 = (bf16[256,128]{1,0:T(8,128)(2,1)S(1)}, f32[256]{0:T(256)S(1)}) all-reduce(f32[256,128]{1,0:T(8,128)S(1)} %convolution_bitcast_fusion.3, f32[256]{0:T(256)S(1)} %bitcast.597), channel_id=1, replica_groups=mesh['space'=4,'member'=4,'lag'=2] {'space','lag'}, use_global_device_ids=true, to_apply=%region_0.1 | all-reduce | flops 33024 | bytes 198656 | tf_op jit(solution)/shard_map/psum | solution.py:70
  57.4 9.3 %all_gather.25 = bf16[256,512]{1,0:T(8,128)(2,1)S(1)} all-gather(bf16[256,128]{1,0:T(8,128)(2,1)S(1)} %get-tuple-element.261), channel_id=1, replica_groups=mesh['space'=4,'member'=4,'lag'=2] {'member'}, dimensions={1}, use_global_device_ids=true | all-gather | bytes 327680 | tf_op jit(solution)/shard_map/all_gather | solution.py:72
  66.8 8.5 %all-reduce.5 = (f32[4,256]{1,0:T(4,128)S(1)}, f32[4,256]{1,0:T(4,128)S(1)}) all-reduce(f32[4,256]{1,0:T(4,128)S(1)} %get-tuple-element.318, f32[4,256]{1,0:T(4,128)S(1)} %get-tuple-element.317), channel_id=1, replica_groups=mesh['space'=4,'member'=4,'lag'=2] {'space'}, use_global_device_ids=true, to_apply=%region_1.2 | all-reduce | flops 2048 | bytes 16384 | tf_op jit(solution)/shard_map/psum | solution.py:52
  76.4 11.7 %cholesky.214 = f32[128,128]{1,0:T(8,128)S(1)} custom-call(f32[128,128]{1,0:T(8,128)S(1)} %cholesky.346), custom_call_target="Cholesky" | custom-call | tf_op jit(solution)/shard_map/jit(cholesky)/cholesky | solution.py:12
  88.3 9.8 %custom-call.35 = f32[1,128,128]{1,2,0:T(8,128)S(1)} custom-call(f32[1,128,128]{2,1,0:T(8,128)S(1)} %get-tuple-element.296), custom_call_target="InvertDiagBlocksLowerTriangular" | custom-call | tf_op jit(solution)/shard_map/jit(cholesky)/cholesky | solution.py:12
  98.7 11.7 %cholesky.231 = f32[128,128]{1,0:T(8,128)S(1)} custom-call(f32[128,128]{1,0:T(8,128)S(1)} %convolution_subtract_fusion.15), custom_call_target="Cholesky" | custom-call | tf_op jit(solution)/shard_map/jit(cholesky)/cholesky | solution.py:12
  113.5 5.0 while.32
  118.6 4.4 while.33
  127.2 19.7 %custom-call.36 = f32[2,128,128]{1,2,0:T(8,128)S(1)} custom-call(f32[2,128,128]{2,1,0:T(8,128)S(1)} %get-tuple-element.111), custom_call_target="InvertDiagBlocksLowerTriangular" | custom-call | tf_op jit(solution)/shard_map/triangular_solve/custom-call.0 | solution.py:14
  146.9 19.7 %custom-call.37 = f32[2,128,128]{1,2,0:T(8,128)S(1)} custom-call(f32[2,128,128]{2,1,0:T(8,128)S(1)} %get-tuple-element.112), custom_call_target="InvertDiagBlocksLowerTriangular" | custom-call | tf_op jit(solution)/shard_map/triangular_solve/custom-call.4 | solution.py:17
  174.1 2.4 fusion.66
  176.5 1.8 multiply_convert_fusion.3
  179.6 1.7 scatter_fusion
  181.3 1.5 gather_fusion.1
  182.9 1.9 convolution_bitcast_fusion.2
  184.8 3.1 fusion.162
  190.3 1.6 fusion.26
  192.0 28.0 %all-reduce.11 = (bf16[256,128]{1,0:T(8,128)(2,1)S(1)}, f32[256]{0:T(256)S(1)}) all-reduce(f32[256,128]{1,0:T(8,128)S(1)} %convolution_bitcast_fusion.2, f32[256]{0:T(256)S(1)} %bitcast.594), channel_id=1, replica_groups=mesh['space'=4,'member'=4,'lag'=2] {'space','lag'}, use_global_device_ids=true, to_apply=%region_7.11 | all-reduce | flops 33024 | bytes 198656 | tf_op jit(solution)/shard_map/psum | solution.py:70
  220.6 8.9 %all_gather.27 = bf16[256,512]{1,0:T(8,128)(2,1)S(1)} all-gather(bf16[256,128]{1,0:T(8,128)(2,1)S(1)} %get-tuple-element.259), channel_id=1, replica_groups=mesh['space'=4,'member'=4,'lag'=2] {'member'}, dimensions={1}, use_global_device_ids=true | all-gather | bytes 327680 | tf_op jit(solution)/shard_map/all_gather | solution.py:72
  231.4 11.7 %cholesky.248 = f32[128,128]{1,0:T(8,128)S(1)} custom-call(f32[128,128]{1,0:T(8,128)S(1)} %cholesky.349), custom_call_target="Cholesky" | custom-call | tf_op jit(solution)/shard_map/jit(cholesky)/cholesky | solution.py:12
  243.2 9.8 %custom-call.38 = f32[1,128,128]{1,2,0:T(8,128)S(1)} custom-call(f32[1,128,128]{2,1,0:T(8,128)S(1)} %get-tuple-element.294), custom_call_target="InvertDiagBlocksLowerTriangular" | custom-call | tf_op jit(solution)/shard_map/jit(cholesky)/cholesky | solution.py:12
  253.6 11.7 %cholesky.265 = f32[128,128]{1,0:T(8,128)S(1)} custom-call(f32[128,128]{1,0:T(8,128)S(1)} %convolution_subtract_fusion.14), custom_call_target="Cholesky" | custom-call | tf_op jit(solution)/shard_map/jit(cholesky)/cholesky | solution.py:12
  268.2 4.4 while.34
  272.7 4.2 while.35
  276.9 19.7 %custom-call.39 = f32[2,128,128]{1,2,0:T(8,128)S(1)} custom-call(f32[2,128,128]{2,1,0:T(8,128)S(1)} %get-tuple-element.113), custom_call_target="InvertDiagBlocksLowerTriangular" | custom-call | tf_op jit(solution)/shard_map/triangular_solve/custom-call.0 | solution.py:14
  296.6 19.7 %custom-call.40 = f32[2,128,128]{1,2,0:T(8,128)S(1)} custom-call(f32[2,128,128]{2,1,0:T(8,128)S(1)} %get-tuple-element.114), custom_call_target="InvertDiagBlocksLowerTriangular" | custom-call | tf_op jit(solution)/shard_map/triangular_solve/custom-call.4 | solution.py:17
  320.8 2.4 fusion.63
  323.2 1.8 multiply_convert_fusion.2
  326.3 1.7 scatter_fusion.1
  328.0 1.5 gather_fusion.2
  329.6 1.9 convolution_bitcast_fusion.1
  331.5 3.1 fusion.165
  336.9 1.6 fusion.23
  338.5 28.0 %all-reduce.12 = (bf16[256,128]{1,0:T(8,128)(2,1)S(1)}, f32[256]{0:T(256)S(1)}) all-reduce(f32[256,128]{1,0:T(8,128)S(1)} %convolution_bitcast_fusion.1, f32[256]{0:T(256)S(1)} %bitcast.595), channel_id=1, replica_groups=mesh['space'=4,'member'=4,'lag'=2] {'space','lag'}, use_global_device_ids=true, to_apply=%region_9.13 | all-reduce | flops 33024 | bytes 198656 | tf_op jit(solution)/shard_map/psum | solution.py:70
  367.2 8.3 %all_gather.29 = bf16[256,512]{1,0:T(8,128)(2,1)S(1)} all-gather(bf16[256,128]{1,0:T(8,128)(2,1)S(1)} %get-tuple-element.257), channel_id=1, replica_groups=mesh['space'=4,'member'=4,'lag'=2] {'member'}, dimensions={1}, use_global_device_ids=true | all-gather | bytes 327680 | tf_op jit(solution)/shard_map/all_gather | solution.py:72
  377.3 11.7 %cholesky.282 = f32[128,128]{1,0:T(8,128)S(1)} custom-call(f32[128,128]{1,0:T(8,128)S(1)} %cholesky.352), custom_call_target="Cholesky" | custom-call | tf_op jit(solution)/shard_map/jit(cholesky)/cholesky | solution.py:12
  389.2 9.8 %custom-call.41 = f32[1,128,128]{1,2,0:T(8,128)S(1)} custom-call(f32[1,128,128]{2,1,0:T(8,128)S(1)} %get-tuple-element.292), custom_call_target="InvertDiagBlocksLowerTriangular" | custom-call | tf_op jit(solution)/shard_map/jit(cholesky)/cholesky | solution.py:12
  399.6 11.7 %cholesky.299 = f32[128,128]{1,0:T(8,128)S(1)} custom-call(f32[128,128]{1,0:T(8,128)S(1)} %convolution_subtract_fusion.13), custom_call_target="Cholesky" | custom-call | tf_op jit(solution)/shard_map/jit(cholesky)/cholesky | solution.py:12
  414.1 4.3 while.36
  418.4 4.1 while.37
  422.6 19.7 %custom-call.42 = f32[2,128,128]{1,2,0:T(8,128)S(1)} custom-call(f32[2,128,128]{2,1,0:T(8,128)S(1)} %get-tuple-element.115), custom_call_target="InvertDiagBlocksLowerTriangular" | custom-call | tf_op jit(solution)/shard_map/triangular_solve/custom-call.0 | solution.py:14
  442.3 19.7 %custom-call.43 = f32[2,128,128]{1,2,0:T(8,128)S(1)} custom-call(f32[2,128,128]{2,1,0:T(8,128)S(1)} %get-tuple-element.116), custom_call_target="InvertDiagBlocksLowerTriangular" | custom-call | tf_op jit(solution)/shard_map/triangular_solve/custom-call.4 | solution.py:17
  466.4 2.4 fusion.60
  468.8 1.8 multiply_convert_fusion.1
  471.9 1.7 scatter_fusion.2
  473.6 1.5 gather_fusion.3
  475.2 1.9 convolution_bitcast_fusion
  477.0 3.1 fusion.168
  482.5 1.6 fusion.20
  484.1 27.8 %all-reduce.13 = (bf16[256,128]{1,0:T(8,128)(2,1)S(1)}, f32[256]{0:T(256)S(1)}) all-reduce(f32[256,128]{1,0:T(8,128)S(1)} %convolution_bitcast_fusion, f32[256]{0:T(256)S(1)} %bitcast.596), channel_id=1, replica_groups=mesh['space'=4,'member'=4,'lag'=2] {'space','lag'}, use_global_device_ids=true, to_apply=%region_11.15 | all-reduce | flops 33024 | bytes 198656 | tf_op jit(solution)/shard_map/psum | solution.py:70
  512.6 8.9 %all_gather.31 = bf16[256,512]{1,0:T(8,128)(2,1)S(1)} all-gather(bf16[256,128]{1,0:T(8,128)(2,1)S(1)} %get-tuple-element.255), channel_id=1, replica_groups=mesh['space'=4,'member'=4,'lag'=2] {'member'}, dimensions={1}, use_global_device_ids=true | all-gather | bytes 327680 | tf_op jit(solution)/shard_map/all_gather | solution.py:72
  522.7 11.7 %cholesky.316 = f32[128,128]{1,0:T(8,128)S(1)} custom-call(f32[128,128]{1,0:T(8,128)S(1)} %cholesky.355), custom_call_target="Cholesky" | custom-call | tf_op jit(solution)/shard_map/jit(cholesky)/cholesky | solution.py:12
  534.5 9.8 %custom-call.44 = f32[1,128,128]{1,2,0:T(8,128)S(1)} custom-call(f32[1,128,128]{2,1,0:T(8,128)S(1)} %get-tuple-element.290), custom_call_target="InvertDiagBlocksLowerTriangular" | custom-call | tf_op jit(solution)/shard_map/jit(cholesky)/cholesky | solution.py:12
  544.9 11.7 %cholesky.333 = f32[128,128]{1,0:T(8,128)S(1)} custom-call(f32[128,128]{1,0:T(8,128)S(1)} %convolution_subtract_fusion.12), custom_call_target="Cholesky" | custom-call | tf_op jit(solution)/shard_map/jit(cholesky)/cholesky | solution.py:12
  559.4 4.6 while.38
  564.0 4.3 while.39
  568.3 19.7 %custom-call.45 = f32[2,128,128]{1,2,0:T(8,128)S(1)} custom-call(f32[2,128,128]{2,1,0:T(8,128)S(1)} %get-tuple-element.117), custom_call_target="InvertDiagBlocksLowerTriangular" | custom-call | tf_op jit(solution)/shard_map/triangular_solve/custom-call.0 | solution.py:14
  588.0 19.7 %custom-call.46 = f32[2,128,128]{1,2,0:T(8,128)S(1)} custom-call(f32[2,128,128]{2,1,0:T(8,128)S(1)} %get-tuple-element.118), custom_call_target="InvertDiagBlocksLowerTriangular" | custom-call | tf_op jit(solution)/shard_map/triangular_solve/custom-call.4 | solution.py:17
  612.2 2.4 fusion.57
  614.6 1.8 multiply_convert_fusion
  617.7 1.7 scatter_fusion.3
  619.4 1.9 fusion.171
  (395 shorter events, 95.7 us)
Async XLA Ops:
  7.2 9.8 %copy-start.57 = (s32[4,1,4]{2,1,0:T(1,128)S(1)}, s32[4,1,4]{2,1,0:T(1,128)}, u32[]{:S(2)}) copy-start(s32[4,1,4]{2,1,0:T(1,128)} %param.21) | copy-start | bytes 196
  7.2 11.3 %copy-start.32 = (s32[4,1,1]{0,2,1:T(1,128)S(1)}, s32[4,1,1]{0,2,1:T(1,128)}, u32[]{:S(2)}) copy-start(s32[4,1,1]{0,2,1:T(1,128)} %param.22) | copy-start | bytes 52
  7.2 1.3 copy-start.33
  7.2 166.9 %all-gather.9.cloned.1.call-start = ((), (), s32[]{:S(2)}) async-start(), calls=%async_computation | async-start | bytes 2621440 | tf_op jit(solution)/shard_map/all_gather | solution.py:74
  8.5 13.8 %copy-start.31 = (f32[1,4096]{1,0:T(1,128)S(1)}, f32[1,4096]{1,0:T(1,128)}, u32[]{:S(2)}) copy-start(f32[1,4096]{1,0:T(1,128)} %param.19) | copy-start | bytes 49156
  17.0 2.2 copy-start.45
  17.0 106.0 %copy-start.43 = (s32[4]{0:T(128)}, s32[4]{0:T(128)S(1)}, u32[]{:S(2)}) copy-start(s32[4]{0:T(128)S(1)} %get-tuple-element.306) | copy-start | bytes 52
  17.0 151.4 %copy-start.41 = (s32[4]{0:T(128)}, s32[4]{0:T(128)S(1)}, u32[]{:S(2)}) copy-start(s32[4]{0:T(128)S(1)} %get-tuple-element.308) | copy-start | bytes 52
  17.0 151.9 %copy-start.39 = (s32[4]{0:T(128)}, s32[4]{0:T(128)S(1)}, u32[]{:S(2)}) copy-start(s32[4]{0:T(128)S(1)} %get-tuple-element.305) | copy-start | bytes 52
  18.4 48.3 %copy-start.59 = (s32[4]{0:T(128)S(1)}, s32[4]{0:T(128)}, u32[]{:S(2)}) copy-start(s32[4]{0:T(128)} %param.25) | copy-start | bytes 52
  18.4 48.3 %copy-start.55 = (f32[1,4,256]{2,1,0:T(4,128)S(1)}, f32[1,4,256]{2,1,0:T(4,128)}, u32[]{:S(2)}) copy-start(f32[1,4,256]{2,1,0:T(4,128)} %param.23) | copy-start | bytes 12292
  18.4 48.3 %copy-start.56 = (f32[1,4,256]{2,1,0:T(4,128)S(1)}, f32[1,4,256]{2,1,0:T(4,128)}, u32[]{:S(2)}) copy-start(f32[1,4,256]{2,1,0:T(4,128)} %param.24) | copy-start | bytes 12292
  18.5 302.3 %all-gather.11.cloned.1.call-start = ((), (), s32[]{:S(2)}) async-start(), calls=%async_computation.1 | async-start | bytes 2621440 | tf_op jit(solution)/shard_map/all_gather | solution.py:74
  19.9 37.5 %copy-start.37 = (pred[4]{0:T(512)(128)(4,1)}, pred[4]{0:T(512)(128)(4,1)S(1)}, u32[]{:S(2)}) copy-start(pred[4]{0:T(512)(128)(4,1)S(1)} %iota_compare_fusion.7) | copy-start | bytes 16
  23.5 33.8 %copy-start.20 = (f32[4,512]{1,0:T(4,128)}, f32[4,512]{1,0:T(4,128)S(1)}, u32[]{:S(2)}) copy-start(f32[4,512]{1,0:T(4,128)S(1)} %gather_fusion.4) | copy-start | bytes 24580
  57.4 18.6 %copy-start.12 = (bf16[256,128]{1,0:T(8,128)(2,1)}, bf16[256,128]{1,0:T(8,128)(2,1)S(1)}, u32[]{:S(2)}) copy-start(bf16[256,128]{1,0:T(8,128)(2,1)S(1)} %get-tuple-element.261) | copy-start | bytes 196612
  66.7 46.7 %copy-start.5 = (bf16[256,512]{1,0:T(8,128)(2,1)}, bf16[256,512]{1,0:T(8,128)(2,1)S(1)}, u32[]{:S(2)}) copy-start(bf16[256,512]{1,0:T(8,128)(2,1)S(1)} %all_gather.25) | copy-start | bytes 786436
  75.9 90.6 %copy-start.29 = (f32[1,256]{1,0:T(1,128)}, f32[1,256]{1,0:T(1,128)S(1)}, u32[]{:S(2)}) copy-start(f32[1,256]{1,0:T(1,128)S(1)} %get-tuple-element.320) | copy-start | bytes 3076
  75.9 91.2 %copy-start.27 = (f32[1,256]{1,0:T(1,128)}, f32[1,256]{1,0:T(1,128)S(1)}, u32[]{:S(2)}) copy-start(f32[1,256]{1,0:T(1,128)S(1)} %get-tuple-element.321) | copy-start | bytes 3076
  75.9 91.8 %copy-start.25 = (f32[1,256]{1,0:T(1,128)}, f32[1,256]{1,0:T(1,128)S(1)}, u32[]{:S(2)}) copy-start(f32[1,256]{1,0:T(1,128)S(1)} %get-tuple-element.322) | copy-start | bytes 3076
  123.0 23.9 %copy-start.60 = (s32[2,2]{1,0:T(2,128)}, s32[2,2]{1,0:T(2,128)S(1)}, u32[]{:S(2)}) copy-start(s32[2,2]{1,0:T(2,128)S(1)} %get-tuple-element.700) | copy-start | bytes 52
  174.1 2.4 copy-start.8
  176.5 1.8 copy-start.1
  176.5 1.8 copy-start.13
  176.5 1.8 copy-start.38
  178.4 1.2 copy-start.46
  182.9 283.5 %all-gather.13.cloned.1.call-start = ((), (), s32[]{:S(2)}) async-start(), calls=%async_computation.2 | async-start | bytes 2621440 | tf_op jit(solution)/shard_map/all_gather | solution.py:74
  189.6 2.4 copy-start.21
  220.0 0.6 copy-start.16
  220.6 47.5 %copy-start.30 = (f32[1,256]{1,0:T(1,128)S(1)}, f32[1,256]{1,0:T(1,128)}, u32[]{:S(2)}) copy-start(f32[1,256]{1,0:T(1,128)} %copy-done.29) | copy-start | bytes 3076
  229.5 0.7 copy-start.6
  231.2 37.0 %copy-start.61 = (s32[2,2]{1,0:T(2,128)S(1)}, s32[2,2]{1,0:T(2,128)}, u32[]{:S(2)}) copy-start(s32[2,2]{1,0:T(2,128)} %copy-done.60) | copy-start | bytes 52
  268.2 48.1 %copy-start.54 = (f32[1,256]{1,0:T(1,128)S(1)}, f32[1,256]{1,0:T(1,128)}, u32[]{:S(2)}) copy-start(f32[1,256]{1,0:T(1,128)} %get-tuple-element.299) | copy-start | bytes 3076
  276.9 43.9 %copy-start.62 = (s32[2,2]{1,0:T(2,128)}, s32[2,2]{1,0:T(2,128)S(1)}, u32[]{:S(2)}) copy-start(s32[2,2]{1,0:T(2,128)S(1)} %get-tuple-element.702) | copy-start | bytes 52
  320.8 2.4 copy-start.9
  323.2 1.8 copy-start.3
  323.2 1.8 copy-start.17
  323.2 1.8 copy-start.36
  325.0 1.2 copy-start.44
  329.5 282.7 %all-gather.15.cloned.1.call-start = ((), (), s32[]{:S(2)}) async-start(), calls=%async_computation.3 | async-start | bytes 2621440 | tf_op jit(solution)/shard_map/all_gather | solution.py:74
  336.2 2.3 copy-start.22
  367.2 46.8 %copy-start.28 = (f32[1,256]{1,0:T(1,128)S(1)}, f32[1,256]{1,0:T(1,128)}, u32[]{:S(2)}) copy-start(f32[1,256]{1,0:T(1,128)} %copy-done.27) | copy-start | bytes 3076
  375.5 0.7 copy-start.7
  377.1 36.9 %copy-start.63 = (s32[2,2]{1,0:T(2,128)S(1)}, s32[2,2]{1,0:T(2,128)}, u32[]{:S(2)}) copy-start(s32[2,2]{1,0:T(2,128)} %copy-done.62) | copy-start | bytes 52
  414.1 47.9 %copy-start.53 = (f32[1,256]{1,0:T(1,128)S(1)}, f32[1,256]{1,0:T(1,128)}, u32[]{:S(2)}) copy-start(f32[1,256]{1,0:T(1,128)} %get-tuple-element.298) | copy-start | bytes 3076
  422.6 43.8 %copy-start.64 = (s32[2,2]{1,0:T(2,128)}, s32[2,2]{1,0:T(2,128)S(1)}, u32[]{:S(2)}) copy-start(s32[2,2]{1,0:T(2,128)S(1)} %get-tuple-element.704) | copy-start | bytes 52
  466.4 2.4 copy-start.10
  468.8 1.8 copy-start.4
  468.8 1.8 copy-start.19
  468.8 1.8 copy-start.35
  470.7 1.2 copy-start.42
  481.7 2.3 copy-start.23
  512.6 46.7 %copy-start.26 = (f32[1,256]{1,0:T(1,128)S(1)}, f32[1,256]{1,0:T(1,128)}, u32[]{:S(2)}) copy-start(f32[1,256]{1,0:T(1,128)} %copy-done.25) | copy-start | bytes 3076
  522.4 36.9 %copy-start.65 = (s32[2,2]{1,0:T(2,128)S(1)}, s32[2,2]{1,0:T(2,128)}, u32[]{:S(2)}) copy-start(s32[2,2]{1,0:T(2,128)} %copy-done.64) | copy-start | bytes 52
  559.3 48.3 %copy-start.52 = (f32[1,256]{1,0:T(1,128)S(1)}, f32[1,256]{1,0:T(1,128)}, u32[]{:S(2)}) copy-start(f32[1,256]{1,0:T(1,128)} %get-tuple-element.297) | copy-start | bytes 3076
  612.2 2.4 copy-start.11
  614.6 1.9 copy-start.2
  614.6 1.9 copy-start.15
  614.6 1.9 copy-start.34
  614.6 3.1 copy-start.40
  616.5 2.9 copy-start.51
  616.5 2.9 copy-start.58
  617.7 3.6 copy-start.24
  619.4 3.2 copy-start
  (6 other events, 3.5 us)
Sparse Core Ops, SparseCore 0:
  18.6 37.8 all-gather.8
  183.0 33.8 all-gather.10
  329.7 32.3 all-gather.12
  475.3 32.4 all-gather.14
where the time goes:
time: 640 us; the launch traced here: 630 us
  other arithmetic  311 us (49%)
  blocking collectives  160 us (25%)
  matrix products  68 us (11%)
  local copies, waits for them, and re-layouts  60.2 us (9%)
  between operations  28.7 us (4%)
    another operation x28, other arithmetic, innovation(): factor = jnp.linalg.cholesky(innov_cov)  139 us
    psum x4, blocking collectives, body(): obs_anoms, obs_means = lax.psum((part_anoms, part_means), ('space', 'lag'))  116 us
    another operation x9, other arithmetic, innovation(): lax.linalg.triangular_solve(factor, inverse_sum, left_side=True, lower=Tr...  78.9 us
    another operation x4, other arithmetic, innovation(): lax.linalg.triangular_solve(factor + jnp.diag(errors_now), identity, left...  78.7 us
    all_gather x4, blocking collectives, body(): obs_round = lax.all_gather(own_round, 'member', axis=1, tiled=True)  35.5 us
    another operation x40, local copies, waits for them, and re-layouts, innovation(): lax.linalg.triangular_solve(factor + jnp.diag(errors_now), identity, left...  16.9 us
    another operation x49, local copies, waits for them, and re-layouts, innovation(): lax.linalg.triangular_solve(factor, inverse_sum, left_side=True, lower=Tr...  16.9 us
  transfers between devices with their start and end apart: 4, of which 0 were waited for; matrix products, arithmetic and copies ran while one was open for 63% of the time, Pallas kernels for 0%

commit v1 on v0

v1 whole, which is shorter than its diff:
```python
import functools

import jax
import jax.numpy as jnp
from jax import lax
from jax.experimental import pallas as pl
from jax.experimental.pallas import tpu as pltpu
from jax.sharding import PartitionSpec as P

HIGH = lax.Precision.HIGHEST
BF = jnp.bfloat16
F32 = jnp.float32
BLK = 64


def prints_kernel(order, tiles, dest, f_ref, x_ref, p_ref, m_ref, acc):
    step = pl.program_id(0)

    @pl.when(step == 0)
    def _():
        acc[...] = jnp.zeros_like(acc)

    part = jnp.dot(f_ref[0, 0], x_ref[0], preferred_element_type=F32)
    acc[dest[step]] += part

    @pl.when(step == pl.num_programs(0) - 1)
    def _():
        count = p_ref.shape[0]
        p_ref[...] = acc[:count, :, : p_ref.shape[2]].astype(BF)
        m_ref[...] = acc[:count, :, p_ref.shape[2] :]


def factor(block, errs):
    lanes = lax.broadcasted_iota(jnp.int32, (1, 2 * BLK), 1)
    a = block
    both_row = lax.broadcasted_iota(jnp.int32, (BLK, 2 * BLK), 0)
    both_col = lax.broadcasted_iota(jnp.int32, (BLK, 2 * BLK), 1)
    both = jnp.where(lax.rem(both_col, BLK) == both_row, 1.0, 0.0).astype(F32)
    done = []
    for group in range(BLK // 8):
        rows = BLK - 8 * group
        row_id = lax.broadcasted_iota(jnp.int32, (rows, 1), 0)
        row_wide = lax.broadcasted_iota(jnp.int32, (rows, 2 * BLK), 0)
        for i in range(8):
            k = 8 * group + i
            pivot = a[i : i + 1, k : k + 1]
            root = lax.rsqrt(pivot)
            below = jnp.where(row_id > i, a[:, k : k + 1] * root, 0.0)
            row = a[i : i + 1, :] * root
            scale = jnp.where(lanes < BLK, root, 1.0 / (pivot * root + errs[k : k + 1, :]))
            both_k = both[i : i + 1, :] * scale
            a = a - below * row
            both = jnp.where(row_wide == i, both_k, both - below * both_k)
        done.append(both[:8])
        a = a[8:]
        both = both[8:]
    full = jnp.concatenate(done, axis=0)
    return full[:, :BLK], full[:, BLK:]


def chain_kernel(
    own_ref, p_ref, m_ref, val_ref, err_ref, c_ref, ps, ms, qs, cov, inv, inv_sum
):
    batches = pl.num_programs(0)
    total = 4
    k_now = pl.program_id(0)
    groups, mats, obs, width = p_ref.shape
    members = groups * width

    @pl.when(k_now == 0)
    def _():
        for g in range(groups):
            ps[:, :, g * width : (g + 1) * width] = p_ref[g]
        ms[...] = m_ref[...]

    here = lax.shift_left(1, k_now) - 1
    y = ps[here]
    errs = err_ref[0]
    rows = lax.broadcasted_iota(jnp.int32, (obs, obs), 0)
    cols = lax.broadcasted_iota(jnp.int32, (obs, obs), 1)
    gram = lax.dot_general(y, y, (((1,), (1,)), ((), ())), preferred_element_type=F32)
    cov[...] = gram / (members - 1) + jnp.where(rows == cols, errs * errs, 0.0)
    unit = jnp.where(rows == cols, 1.0, 0.0).astype(F32)
    inv[...] = unit
    inv_sum[...] = unit
    lane = lax.broadcasted_iota(jnp.int32, (BLK, obs), 1)

    def block_step(j, carry):
        at = pl.ds(pl.multiple_of(j * BLK, BLK), BLK)
        strip = cov[at, :]
        diag = strip[:, :BLK]
        for c in range(1, obs // BLK):
            diag = jnp.where(j == c, strip[:, c * BLK : (c + 1) * BLK], diag)
        low, low_sum = factor(diag, err_ref[0, at, :])
        upper = jnp.dot(low, strip, precision=HIGH, preferred_element_type=F32)
        upper = jnp.where(lane >= (j + 1) * BLK, upper, 0.0)
        row_inv = jnp.dot(low, inv[at, :], precision=HIGH, preferred_element_type=F32)
        row_sum = jnp.dot(low_sum, inv_sum[at, :], precision=HIGH, preferred_element_type=F32)
        inv[at, :] = row_inv
        inv_sum[at, :] = row_sum
        wide = jnp.concatenate([upper, row_inv, row_sum], axis=1)
        drop = jnp.dot(upper.T, wide, precision=HIGH, preferred_element_type=F32)
        cov[...] -= drop[:, :obs]
        inv[...] -= drop[:, obs : 2 * obs]
        inv_sum[...] -= drop[:, 2 * obs :]
        return carry

    lax.fori_loop(0, obs // BLK, block_step, 0)
    lower_inv = inv[...]
    miss = ms[here] - val_ref[0]
    right = jnp.concatenate(
        [
            jnp.dot(inv_sum[...], y.astype(F32), precision=HIGH, preferred_element_type=F32),
            jnp.dot(lower_inv, miss, precision=HIGH, preferred_element_type=F32),
        ],
        axis=1,
    )
    weights = jnp.dot(lower_inv.T, right, precision=HIGH, preferred_element_type=F32)
    q = lax.dot_general(
        y, weights.astype(BF), (((0,), (0,)), ((), ())), preferred_element_type=F32
    ) / (members - 1)
    qs[k_now] = q.astype(BF)

    for k in range(total - 1):

        @pl.when(k_now == k)
        def _(k=k):
            qk = qs[k]
            for b in range(k + 1, total):
                base = 2**b - 1
                for s in range(0, 2**b, 2 ** (k + 1)):
                    keep, move = base + s, base + s + 2**k
                    source = ps[move]
                    change = jnp.dot(source, qk, preferred_element_type=F32)
                    ps[keep] = (
                        ps[keep].astype(F32) + source.astype(F32) - change[:, :members]
                    ).astype(BF)
                    ms[keep] = ms[keep] + ms[move] - change[:, members:]

    @pl.when(k_now == batches - 1)
    def _():
        c_ref[0] = jnp.zeros(c_ref.shape[1:], BF)
        own = pl.ds(pl.multiple_of(own_ref[0] * width, width), width)
        for k in range(total - 1, -1, -1):
            term = jnp.concatenate([qs[k, :, own], qs[k, :, members:]], axis=1)
            c_ref[2**k] = term
            for s in range(2 ** (k + 1), 2**total, 2 ** (k + 1)):
                prior = c_ref[s]
                c_ref[s + 2**k] = (
                    prior.astype(F32)
                    + term.astype(F32)
                    - jnp.dot(qs[k, :, :members], prior, preferred_element_type=F32)
                ).astype(BF)


def final_kernel(history, x_ref, all_ref, mean_ref, c_ref, out_ref, mean_out):
    groups, _, width = all_ref.shape
    change = jnp.zeros((x_ref.shape[1], 2 * width), F32)
    for g in range(groups):
        change += jnp.dot(
            all_ref[g], c_ref[0, g * width : (g + 1) * width, :], preferred_element_type=F32
        )
    out_ref[0] = (x_ref[0].astype(F32) - change[:, :width]).astype(BF)
    shift = change[:, width:].T[0:1, :]
    mean_out[0] = mean_ref[0] - shift


def body(
    anomalies,
    mean_state,
    footprints,
    slot_tiles,
    slot_counts,
    obs_values,
    obs_errors,
    owners,
    batch_order,
):
    batches, _, slot_dev, obs, tile_cells = footprints.shape
    width = anomalies.shape[2]
    groups = lax.axis_size("member")
    members = width * groups
    tiles = anomalies.shape[1] // tile_cells
    mats = 2**batches - 1
    x = anomalies[0].reshape(tiles, tile_cells, width)
    means = mean_state[0].reshape(tiles, 1, tile_cells)
    x_all = lax.all_gather(anomalies[0], "member", axis=0)

    ids = slot_tiles[:, 0][batch_order]
    counts = slot_counts[:, 0, 0][batch_order]
    live = jnp.arange(slot_dev)[None, :] < counts[:, None]
    tile_live = jnp.any(
        (ids[:, :, None] == jnp.arange(tiles)) & live[:, :, None], axis=1
    ).astype(jnp.int32)
    bits = jnp.left_shift(1, jnp.arange(batches))[:, None] * tile_live
    history = jnp.sum(bits, axis=0)
    before = jnp.cumsum(bits, axis=0) - bits
    slot_before = jnp.take_along_axis(before, ids, axis=1)
    base = (jnp.left_shift(1, jnp.arange(batches)) - 1)[:, None]
    dest = jnp.where(live, base + slot_before, mats).astype(jnp.int32).reshape(-1)

    mean_pad = jnp.pad(
        mean_state[0].astype(BF).reshape(tiles, tile_cells, 1), ((0, 0), (0, 0), (0, width - 1))
    )
    x_mean = jnp.concatenate([x, mean_pad], axis=2)
    part, part_mean = pl.pallas_call(
        prints_kernel,
        out_shape=(
            jax.ShapeDtypeStruct((mats, obs, width), BF),
            jax.ShapeDtypeStruct((mats, obs, width), F32),
        ),
        grid_spec=pltpu.PrefetchScalarGridSpec(
            num_scalar_prefetch=3,
            grid=(batches * slot_dev,),
            in_specs=[
                pl.BlockSpec(
                    (1, 1, obs, tile_cells),
                    lambda i, o, t, d: (o[i // slot_dev], i % slot_dev, 0, 0),
                ),
                pl.BlockSpec((1, tile_cells, 2 * width), lambda i, o, t, d: (t[i], 0, 0)),
            ],
            out_specs=[
                pl.BlockSpec((mats, obs, width), lambda i, o, t, d: (0, 0, 0)),
                pl.BlockSpec((mats, obs, width), lambda i, o, t, d: (0, 0, 0)),
            ],
            scratch_shapes=[pltpu.VMEM((mats + 1, obs, 2 * width), F32)],
        ),
        compiler_params=pltpu.CompilerParams(vmem_limit_bytes=40 * 2**20),
        name="prints",
    )(batch_order, ids.reshape(-1), dest, footprints[:, 0], x_mean)

    small = jnp.concatenate(
        [part_mean[:, :, 0], obs_values[0], obs_errors[0]], axis=0
    )
    small_all = lax.all_gather(small, ("space", "lag"), axis=0)
    mean_sum = jnp.sum(small_all[:, :mats], axis=0)
    lags = lax.axis_size("lag")
    owner_row = owners[batch_order] * lags
    values = small_all[owner_row, mats + batch_order]
    errors = small_all[owner_row, mats + batches + batch_order]

    summed = lax.psum(part, ("space", "lag"))
    p_all = lax.all_gather(summed, "member", axis=0)
    own = lax.axis_index("member").astype(jnp.int32).reshape(1)
    mean_cols = jnp.pad(mean_sum[:, :, None], ((0, 0), (0, 0), (0, width - 1)))

    states = pl.pallas_call(
        chain_kernel,
        out_shape=jax.ShapeDtypeStruct((2**batches, members, 2 * width), BF),
        grid_spec=pltpu.PrefetchScalarGridSpec(
            num_scalar_prefetch=1,
            grid=(batches,),
            in_specs=[
                pl.BlockSpec((groups, mats, obs, width), lambda k, o: (0, 0, 0, 0)),
                pl.BlockSpec((mats, obs, width), lambda k, o: (0, 0, 0)),
                pl.BlockSpec((1, obs, 1), lambda k, o: (k, 0, 0)),
                pl.BlockSpec((1, obs, 1), lambda k, o: (k, 0, 0)),
            ],
            out_specs=pl.BlockSpec(
                (2**batches, members, 2 * width), lambda k, o: (0, 0, 0)
            ),
            scratch_shapes=[
                pltpu.VMEM((mats, obs, members), BF),
                pltpu.VMEM((mats, obs, width), F32),
                pltpu.VMEM((batches, members, members + width), BF),
                pltpu.VMEM((obs, obs), F32),
                pltpu.VMEM((obs, obs), F32),
                pltpu.VMEM((obs, obs), F32),
            ],
        ),
        compiler_params=pltpu.CompilerParams(vmem_limit_bytes=56 * 2**20),
        cost_estimate=pl.CostEstimate(
            flops=20 * 10**9, bytes_accessed=10**7, transcendentals=0
        ),
        name="chain",
    )(own, p_all, mean_cols, values[:, :, None], errors[:, :, None])

    new_x, new_mean = pl.pallas_call(
        final_kernel,
        out_shape=(
            jax.ShapeDtypeStruct((tiles, tile_cells, width), BF),
            jax.ShapeDtypeStruct((tiles, 1, tile_cells), F32),
        ),
        grid_spec=pltpu.PrefetchScalarGridSpec(
            num_scalar_prefetch=1,
            grid=(tiles,),
            in_specs=[
                pl.BlockSpec((1, tile_cells, width), lambda t, h: (t, 0, 0)),
                pl.BlockSpec((groups, tile_cells, width), lambda t, h: (0, t, 0)),
                pl.BlockSpec((1, 1, tile_cells), lambda t, h: (t, 0, 0)),
                pl.BlockSpec((1, members, 2 * width), lambda t, h: (h[t], 0, 0)),
            ],
            out_specs=[
                pl.BlockSpec((1, tile_cells, width), lambda t, h: (t, 0, 0)),
                pl.BlockSpec((1, 1, tile_cells), lambda t, h: (t, 0, 0)),
            ],
        ),
        name="final",
    )(history, x, x_all, means, states)
    return (new_x.reshape(1, -1, width), new_mean.reshape(1, -1))


def solution(mesh):
    return jax.shard_map(
        body,
        mesh=mesh,
        in_specs=(
            P("lag", "space", "member"),
            P("lag", "space"),
            P(None, "lag", "space", None, None),
            P(None, "lag", "space"),
            P(None, "lag", "space"),
            P("space", None, None),
            P("space", None, None),
            P(),
            P(),
        ),
        out_specs=(P("lag", "space", "member"), P("lag", "space")),
        check_vma=False,
    )
```

time: 640 us -> 276 us (0.43); the launches traced: 630 us -> 276 us
  other arithmetic: 311 us -> 2.94 us
  blocking collectives: 160 us -> 14.3 us
  Pallas kernels: 0 us -> 139 us
  waiting for transfers between devices: 0.07 us -> 91.6 us
  matrix products: 68 us -> 0 us
  local copies, waits for them, and re-layouts: 60.2 us -> 13.4 us
  between operations: 28.7 us -> 13.9 us
    another operation x41 -> x1, other arithmetic: 296 us -> 0.04 us  [body(): before = jnp.cumsum(bits, axis=0) - bits]
    pallas_call x0 -> x3, Pallas kernels: none -> 139 us  [the longest x1 125 us: body(): pl.pallas_call(chain_kernel, out_shape=jax.ShapeDtypeStruct((2 ** batches...]
    psum x5 -> x0, blocking collectives: 125 us -> none  [the longest x4 116 us: body(): obs_anoms, obs_means = lax.psum((part_anoms, part_means), ('space', 'lag'))]
    psum x0 -> x1, waiting for transfers between devices: none -> 61.1 us  [body(): summed = lax.psum(part, ('space', 'lag'))]
    dot_general x28 -> x0, matrix products: 49.7 us -> none  [the longest x4 11.2 us: body(): jnp.einsum('stp,p->st', covariance, weights_obs, precision=highest)]
    another operation x118 -> x0, local copies, waits for them, and re-layouts: 35.1 us -> none  [the longest x40 16.9 us: innovation(): lax.linalg.triangular_solve(factor + jnp.diag(errors_now), identity, left...]
    all_gather x4 -> x2, waiting for transfers between devices: 0.01 us -> 29.8 us  [the longest x1 29.8 us: body(): p_all = lax.all_gather(summed, 'member', axis=0)]
    all_gather x4 -> x1, blocking collectives: 35.5 us -> 14.3 us  [body(): small_all = lax.all_gather(small, ('space', 'lag'), axis=0)]
  transfers between devices with their start and end apart: 4 -> 3, of which waited for: 0 -> 2; matrix products, arithmetic and copies ran while one was open for 63% -> 2% of each run, Pallas kernels for 0% -> 45%
where the time goes in v1:
time: 276 us
  Pallas kernels  139 us (50%)
  waiting for transfers between devices  91.6 us (33%)
  blocking collectives  14.3 us (5%)
  between operations  13.9 us (5%)
  local copies, waits for them, and re-layouts  13.4 us (5%)
  other arithmetic  2.94 us (1%)
    pallas_call x1, Pallas kernels, body(): pl.pallas_call(chain_kernel, out_shape=jax.ShapeDtypeStruct((2 ** batches...  125 us
    psum x1, waiting for transfers between devices, body(): summed = lax.psum(part, ('space', 'lag'))  61.1 us
    all_gather x1, waiting for transfers between devices, body(): p_all = lax.all_gather(summed, 'member', axis=0)  29.8 us
    all_gather x1, blocking collectives, body(): small_all = lax.all_gather(small, ('space', 'lag'), axis=0)  14.3 us
    pallas_call x1, Pallas kernels, body(): pl.pallas_call(final_kernel, out_shape=(jax.ShapeDtypeStruct((tiles, tile...  8.58 us
    pallas_call x1, Pallas kernels, body(): pl.pallas_call(prints_kernel, out_shape=(jax.ShapeDtypeStruct((mats, obs,...  6.05 us
  transfers between devices with their start and end apart: 3, of which 2 were waited for; matrix products, arithmetic and copies ran while one was open for 2% of the time, Pallas kernels for 45%

profile of v1, /device:TPU:0, one launch (start us, length us, event | category | flops | bytes accessed | tf_op | source)
XLA Modules:
  0.0 275.7 jit_solution(16535612877783318113)
XLA Ops:
  7.2 0.0 copy-start
  7.2 0.0 copy-start.4
  7.2 0.0 all-reduce.4.cloned.1.call-start
  7.2 0.7 compare_select_fusion.5
  8.0 0.0 copy-done
  8.0 0.6 gather_fusion
  8.6 0.1 reshape.103.tiles
  8.7 1.3 gather_fusion.1
  9.9 0.1 iota_compare_fusion.2
  10.0 0.1 fusion.3
  10.1 0.1 lt.63
  10.2 0.1 broadcast_select_fusion
  10.3 0.6 select_subtract_fusion
  10.9 0.1 reshape.142
  11.0 0.1 add.75
  11.1 0.1 add.76
  11.2 0.8 convert_reduce_fusion
  12.0 2.1 convert_element_type.20
  14.1 0.7 gather_fusion.5
  14.8 0.0 copy-done.4
  14.8 0.0 copy-start.1
  14.8 0.0 copy-start.2
  14.8 0.5 fusion.1.x_ref
  15.3 1.7 copy-done.1
  17.0 0.0 copy-done.2
  17.0 6.1 %prints.1 = (bf16[15,256,128]{2,1,0:T(8,128)(2,1)}, f32[15,256,128]{2,1,0:T(8,128)S(1)}) custom-call(s32[4]{0:T(128)S(1)} %copy-done.2, s32[16]{0:T(128)S(1)} %reshape.103.tiles, s32[16]{0:T(128)S(1)} %fusion.14.dest, bf16[4,4,256,512]{3,2,1,0:T(8,128)(2,1)S(1)} %bitcast.39, bf16[8,512,256]{2,1,0:T(8,128)(2,1)S(1)} %fusion.1.x_ref), custom_call_target="tpu_custom_call" | custom-call | tf_op jit(solution)/shard_map/prints/pallas_call | solution.py:206
  23.0 0.0 all-reduce.4.cloned.1.call-update
  23.0 0.0 copy-start.5
  23.1 0.0 copy-start.6
  23.1 0.0 all-gather.7.cloned.1.call-start
  23.1 61.1 %all-reduce.4.cloned.1.call-done = bf16[1,15,256,128]{3,2,1,0:T(8,128)(2,1)} async-done(((bf16[1,15,256,128]{3,2,1,0:T(8,128)(2,1)}), bf16[1,15,256,128]{3,2,1,0:T(8,128)(2,1)}) %all-reduce.4.cloned.1.call-update) | async-done | bytes 983056 | tf_op jit(solution)/shard_map/psum | solution.py:242
  84.2 0.0 copy-start.3
  84.2 0.0 all-gather.7.cloned.1.call-update
  84.2 0.0 all-gather.5.cloned.1.call-start
  84.3 0.7 all-gather.5.cloned.1.call-update
  85.0 0.6 slice_reduce_fusion
  85.6 0.0 copy-done.5
  85.6 0.0 copy-done.6
  85.6 14.3 %all-gather.1 = f32[8,23,256]{2,1,0:T(8,128)S(1)} all-gather(f32[1,23,256]{2,1,0:T(8,128)S(1)} %maximum_bitcast_fusion), channel_id=2, replica_groups=mesh['space'=4,'member'=4,'lag'=2] {'space','lag'}, dimensions={0}, use_global_device_ids=true | all-gather | bytes 211968 | tf_op jit(solution)/shard_map/all_gather | solution.py:235
  99.8 0.1 copy.25
  99.9 0.0 copy-done.3
  99.9 0.6 gather_fusion.2
  100.6 0.6 gather_fusion.3
  101.1 1.0 copy.27.val_ref
  102.2 0.6 gather_fusion.4
  102.7 1.0 copy.28.err_ref
  103.8 0.6 copy.24
  104.4 1.5 pad.9.m_ref
  105.9 29.8 %all-gather.7.cloned.1.call-done.p_ref = bf16[4,15,256,128]{3,2,1,0:T(8,128)(2,1)} async-done(((bf16[1,15,256,128]{3,2,1,0:T(8,128)(2,1)}), bf16[4,15,256,128]{3,2,1,0:T(8,128)(2,1)}) %all-gather.7.cloned.1.call-update) | async-done | bytes 3932176 | tf_op jit(solution)/shard_map/all_gather | solution.py:243
  135.7 124.8 %chain.1.c_ref = bf16[16,512,256]{2,1,0:T(8,128)(2,1)} custom-call(s32[1]{0:T(128)} %bitcast.4.own_ref, bf16[4,15,256,128]{3,2,1,0:T(8,128)(2,1)} %all-gather.7.cloned.1.call-done.p_ref, f32[15,256,128]{2,1,0:T(8,128)} %pad.9.m_ref, f32[4,256,1]{2,1,0:T(8,128)} %copy.27.val_ref, f32[4,256,1]{2,1,0:T(8,128)} %copy.28.err_ref), custom_call_target="tpu_custom_call" | custom-call | flops 20000000000 | bytes 10000000 | tf_op jit(solution)/shard_map/chain/pallas_call | solution.py:247
  260.6 0.0 all-gather.5.cloned.1.call-done.all_ref
  260.6 8.6 %final.1 = (bf16[8,512,128]{2,1,0:T(8,128)(2,1)}, f32[8,1,512]{2,1,0:T(1,128)}) custom-call(s32[8]{0:T(128)} %get-tuple-element.13.history, bf16[8,512,128]{2,1,0:T(8,128)(2,1)} %bitcast.41, bf16[4,4096,128]{2,1,0:T(8,128)(2,1)} %all-gather.5.cloned.1.call-done.all_ref, f32[8,1,512]{2,1,0:T(1,128)} %bitcast.44, bf16[16,512,256]{2,1,0:T(8,128)(2,1)} %chain.1.c_ref), custom_call_target="tpu_custom_call" | custom-call | tf_op jit(solution)/shard_map/final/pallas_call | solution.py:278
  (9 shorter events, 0.1 us)
Async XLA Ops:
  7.2 0.8 copy-start
  7.2 7.6 %copy-start.4 = (bf16[1,4096,128]{2,1,0:T(8,128)(2,1)S(1)}, bf16[1,4096,128]{2,1,0:T(8,128)(2,1)}, u32[]{:S(2)}) copy-start(bf16[1,4096,128]{2,1,0:T(8,128)(2,1)} %param.9) | copy-start | bytes 3145732
  7.2 77.0 %all-reduce.4.cloned.1.call-start = ((), (), s32[]{:S(2)}) async-start(), calls=%async_computation.1 | async-start | bytes 1966080 | tf_op jit(solution)/shard_map/psum | solution.py:242
  14.8 2.2 copy-start.1
  14.8 2.2 copy-start.2
  23.0 62.5 %copy-start.5 = (f32[1,4,256]{2,1,0:T(4,128)S(1)}, f32[1,4,256]{2,1,0:T(4,128)}, u32[]{:S(2)}) copy-start(f32[1,4,256]{2,1,0:T(4,128)} %param.15) | copy-start | bytes 12292
  23.1 62.5 %copy-start.6 = (f32[1,4,256]{2,1,0:T(4,128)S(1)}, f32[1,4,256]{2,1,0:T(4,128)}, u32[]{:S(2)}) copy-start(f32[1,4,256]{2,1,0:T(4,128)} %param.14) | copy-start | bytes 12292
  23.1 112.7 %all-gather.7.cloned.1.call-start = ((), (), s32[]{:S(2)}) async-start(), calls=%async_computation.2 | async-start | bytes 4915200 | tf_op jit(solution)/shard_map/all_gather | solution.py:243
  84.2 15.7 %copy-start.3 = (s32[4]{0:T(128)S(1)}, s32[4]{0:T(128)}, u32[]{:S(2)}) copy-start(s32[4]{0:T(128)} %param.16) | copy-start | bytes 52
  84.2 176.3 %all-gather.5.cloned.1.call-start = ((), (), s32[]{:S(2)}) async-start(), calls=%async_computation | async-start | bytes 5242880 | tf_op jit(solution)/shard_map/all_gather | solution.py:187
Sparse Core Ops, SparseCore 0:
  23.2 60.9 all-reduce.3
  86.2 49.4 all-gather.6
  137.7 52.7 all-gather.4

commit v2 on v1

--- a/solution.py
+++ b/solution.py
@@ -39,18 +39,25 @@
     done = []
     for group in range(BLK // 8):
         rows = BLK - 8 * group
-        row_id = lax.broadcasted_iota(jnp.int32, (rows, 1), 0)
         row_wide = lax.broadcasted_iota(jnp.int32, (rows, 2 * BLK), 0)
-        for i in range(8):
-            k = 8 * group + i
-            pivot = a[i : i + 1, k : k + 1]
-            root = lax.rsqrt(pivot)
-            below = jnp.where(row_id > i, a[:, k : k + 1] * root, 0.0)
-            row = a[i : i + 1, :] * root
-            scale = jnp.where(lanes < BLK, root, 1.0 / (pivot * root + errs[k : k + 1, :]))
-            both_k = both[i : i + 1, :] * scale
-            a = a - below * row
-            both = jnp.where(row_wide == i, both_k, both - below * both_k)
+        for start in range(0, 8, 4):
+            lead = [
+                jnp.broadcast_to(a[:, k : k + 1], (rows, 2 * BLK))
+                for k in range(8 * group + start, 8 * group + start + 4)
+            ]
+            for m in range(4):
+                i = start + m
+                k = 8 * group + i
+                pivot = lead[m][i : i + 1, :]
+                root = lax.rsqrt(pivot)
+                below = jnp.where(row_wide > i, lead[m] * root, 0.0)
+                for n in range(m + 1, 4):
+                    lead[n] = lead[n] - below * below[start + n : start + n + 1, :]
+                row = a[i : i + 1, :] * root[:, :BLK]
+                scale = jnp.where(lanes < BLK, root, 1.0 / (pivot * root + errs[k : k + 1, :]))
+                both_k = both[i : i + 1, :] * scale
+                a = a - below[:, :BLK] * row
+                both = jnp.where(row_wide == i, both_k, both - below * both_k)
         done.append(both[:8])
         a = a[8:]
         both = both[8:]
@@ -239,8 +246,14 @@
     values = small_all[owner_row, mats + batch_order]
     errors = small_all[owner_row, mats + batches + batch_order]
 
-    summed = lax.psum(part, ("space", "lag"))
-    p_all = lax.all_gather(summed, "member", axis=0)
+    summed = lax.psum_scatter(
+        part.reshape(mats * obs, width), ("space", "lag"), scatter_dimension=0, tiled=True
+    )
+    summed, values, errors, mean_sum = lax.optimization_barrier(
+        (summed, values, errors, mean_sum)
+    )
+    p_all = lax.all_gather(summed, ("member", "space", "lag"), axis=0, tiled=True)
+    p_all = p_all.reshape(groups, mats, obs, width)
     own = lax.axis_index("member").astype(jnp.int32).reshape(1)
     mean_cols = jnp.pad(mean_sum[:, :, None], ((0, 0), (0, 0), (0, width - 1)))
 

time: 276 us -> 210 us (0.76)
  Pallas kernels: 139 us -> 87.9 us
  waiting for transfers between devices: 91.6 us -> 75.4 us
    psum x1 -> x0, waiting for transfers between devices: 61.1 us -> none  [body(): summed = lax.psum(part, ('space', 'lag'))]
    pallas_call x1, Pallas kernels: 125 us -> 73.3 us  [body(): pl.pallas_call(chain_kernel, out_shape=jax.ShapeDtypeStruct((2 ** batches...]
    all_gather x1, waiting for transfers between devices: 29.8 us -> 57.9 us  [body(): lax.all_gather(summed, ('member', 'space', 'lag'), axis=0, tiled=True)]
    reduce_scatter x0 -> x1, waiting for transfers between devices: none -> 16.9 us  [body(): lax.psum_scatter(part.reshape(mats * obs, width), ('space', 'lag'), scatt...]
  transfers between devices with their start and end apart: 3 -> 3, of which waited for: 2 -> 2; matrix products, arithmetic and copies ran while one was open for 2% -> 3% of each run, Pallas kernels for 45% -> 35%
where the time goes in v2:
time: 210 us
  Pallas kernels  87.9 us (42%)
  waiting for transfers between devices  75.4 us (36%)
  blocking collectives  16.1 us (8%)
  between operations  13.9 us (7%)
  local copies, waits for them, and re-layouts  13.4 us (6%)
  other arithmetic  2.93 us (1%)
    pallas_call x1, Pallas kernels, body(): pl.pallas_call(chain_kernel, out_shape=jax.ShapeDtypeStruct((2 ** batches...  73.3 us
    all_gather x1, waiting for transfers between devices, body(): lax.all_gather(summed, ('member', 'space', 'lag'), axis=0, tiled=True)  57.9 us
    reduce_scatter x1, waiting for transfers between devices, body(): lax.psum_scatter(part.reshape(mats * obs, width), ('space', 'lag'), scatt...  16.9 us
    all_gather x1, blocking collectives, body(): small_all = lax.all_gather(small, ('space', 'lag'), axis=0)  16.1 us
    pallas_call x1, Pallas kernels, body(): pl.pallas_call(final_kernel, out_shape=(jax.ShapeDtypeStruct((tiles, tile...  8.6 us
    pallas_call x1, Pallas kernels, body(): pl.pallas_call(prints_kernel, out_shape=(jax.ShapeDtypeStruct((mats, obs,...  6.05 us
  transfers between devices with their start and end apart: 3, of which 2 were waited for; matrix products, arithmetic and copies ran while one was open for 3% of the time, Pallas kernels for 35%

profile of v2, /device:TPU:0, one launch (start us, length us, event | category | flops | bytes accessed | tf_op | source)
XLA Modules:
  0.0 209.9 jit_solution(10331480176516193730)
XLA Ops:
  7.2 0.0 copy-start
  7.2 0.0 copy-start.4
  7.2 0.0 reduce-scatter.2.cloned.1.call-start
  7.2 0.7 compare_select_fusion.5
  8.0 0.0 copy-done
  8.0 0.6 gather_fusion
  8.6 0.1 reshape.109.tiles
  8.7 1.3 gather_fusion.1
  9.9 0.1 iota_compare_fusion.2
  10.0 0.1 fusion.3
  10.1 0.1 lt.63
  10.2 0.1 broadcast_select_fusion
  10.3 0.6 select_subtract_fusion
  10.9 0.1 reshape.150
  11.0 0.1 add.75
  11.1 0.1 add.76
  11.2 0.8 convert_reduce_fusion
  12.0 2.1 %convert_element_type.20 = bf16[8,512,1]{2,1,0:T(8,128)(2,1)S(1)} reshape(bf16[4096]{0:T(1024)(128)(2,1)S(1)} %convert_reduce_fusion) | data formatting | bytes 16384 | tf_op jit(solution)/shard_map/convert_element_type | solution.py:210
  14.1 0.7 gather_fusion.5
  14.8 0.0 copy-done.4
  14.8 0.0 copy-start.1
  14.8 0.0 copy-start.2
  14.8 0.5 fusion.1.x_ref
  15.3 1.7 copy-done.1
  17.0 0.0 copy-done.2
  17.0 6.1 %prints.1 = (bf16[15,256,128]{2,1,0:T(8,128)(2,1)}, f32[15,256,128]{2,1,0:T(8,128)S(1)}) custom-call(s32[4]{0:T(128)S(1)} %copy-done.2, s32[16]{0:T(128)S(1)} %reshape.109.tiles, s32[16]{0:T(128)S(1)} %fusion.14.dest, bf16[4,4,256,512]{3,2,1,0:T(8,128)(2,1)S(1)} %bitcast.40, bf16[8,512,256]{2,1,0:T(8,128)(2,1)S(1)} %fusion.1.x_ref), custom_call_target="tpu_custom_call" | custom-call | tf_op jit(solution)/shard_map/prints/pallas_call | solution.py:213
  23.0 0.0 copy-start.5
  23.0 0.0 copy-start.6
  23.0 0.0 copy-start.3
  23.0 0.0 reduce-scatter.2.cloned.1.call-update
  23.1 0.0 all-gather.7.cloned.1.call-start
  23.1 0.6 slice_reduce_fusion
  23.7 0.0 copy-done.5
  23.7 0.0 copy-done.6
  23.7 16.1 %all-gather.1 = f32[8,23,256]{2,1,0:T(8,128)S(1)} all-gather(f32[1,23,256]{2,1,0:T(8,128)S(1)} %maximum_bitcast_fusion), channel_id=2, replica_groups=mesh['space'=4,'member'=4,'lag'=2] {'space','lag'}, dimensions={0}, use_global_device_ids=true | all-gather | bytes 211968 | tf_op jit(solution)/shard_map/all_gather | solution.py:242
  39.8 0.1 copy.24
  39.9 0.0 copy-done.3
  39.9 0.6 gather_fusion.2
  40.5 0.6 gather_fusion.4
  41.1 0.6 gather_fusion.3
  41.7 16.9 %reduce-scatter.2.cloned.1.call-done = bf16[480,128]{1,0:T(8,128)(2,1)} async-done(((bf16[3840,128]{1,0:T(8,128)(2,1)}), bf16[480,128]{1,0:T(8,128)(2,1)}) %reduce-scatter.2.cloned.1.call-update) | async-done | bytes 122896 | tf_op jit(solution)/shard_map/reduce_scatter | solution.py:249
  58.6 0.0 all-gather.7.cloned.1.call-update
  58.6 0.2 all-gather.5.cloned.1.call-start
  58.8 0.5 all-gather.5.cloned.1.call-update
  59.4 0.6 copy.26
  60.0 1.0 copy.27.val_ref
  61.0 1.0 copy.28.err_ref
  62.0 1.5 pad.9.m_ref
  63.5 57.9 %all-gather.7.cloned.1.call-done = bf16[15360,128]{1,0:T(8,128)(2,1)} async-done(((bf16[480,128]{1,0:T(8,128)(2,1)}), bf16[15360,128]{1,0:T(8,128)(2,1)}) %all-gather.7.cloned.1.call-update) | async-done | bytes 3932176 | tf_op jit(solution)/shard_map/all_gather | solution.py:255
  121.5 73.3 %chain.1.c_ref = bf16[16,512,256]{2,1,0:T(8,128)(2,1)} custom-call(s32[1]{0:T(128)} %bitcast.4.own_ref, bf16[4,15,256,128]{3,2,1,0:T(8,128)(2,1)} %bitcast.50, f32[15,256,128]{2,1,0:T(8,128)} %pad.9.m_ref, f32[4,256,1]{2,1,0:T(8,128)} %copy.27.val_ref, f32[4,256,1]{2,1,0:T(8,128)} %copy.28.err_ref), custom_call_target="tpu_custom_call" | custom-call | flops 20000000000 | bytes 10000000 | tf_op jit(solution)/shard_map/chain/pallas_call | solution.py:260
  194.8 0.0 all-gather.5.cloned.1.call-done.all_ref
  194.8 8.6 %final.1 = (bf16[8,512,128]{2,1,0:T(8,128)(2,1)}, f32[8,1,512]{2,1,0:T(1,128)}) custom-call(s32[8]{0:T(128)} %get-tuple-element.21.history, bf16[8,512,128]{2,1,0:T(8,128)(2,1)} %bitcast.42, bf16[4,4096,128]{2,1,0:T(8,128)(2,1)} %all-gather.5.cloned.1.call-done.all_ref, f32[8,1,512]{2,1,0:T(1,128)} %bitcast.45, bf16[16,512,256]{2,1,0:T(8,128)(2,1)} %chain.1.c_ref), custom_call_target="tpu_custom_call" | custom-call | tf_op jit(solution)/shard_map/final/pallas_call | solution.py:291
  (9 shorter events, 0.1 us)
Async XLA Ops:
  7.2 0.8 copy-start
  7.2 7.6 %copy-start.4 = (bf16[1,4096,128]{2,1,0:T(8,128)(2,1)S(1)}, bf16[1,4096,128]{2,1,0:T(8,128)(2,1)}, u32[]{:S(2)}) copy-start(bf16[1,4096,128]{2,1,0:T(8,128)(2,1)} %param.9) | copy-start | bytes 3145732
  7.2 51.4 %reduce-scatter.2.cloned.1.call-start = ((), (), s32[]{:S(2)}) async-start(), calls=%async_computation.2 | async-start | bytes 1105920 | tf_op jit(solution)/shard_map/reduce_scatter | solution.py:249
  14.8 2.2 %copy-start.1 = (bf16[4,1,4,256,512]{4,3,2,1,0:T(8,128)(2,1)S(1)}, bf16[4,1,4,256,512]{4,3,2,1,0:T(8,128)(2,1)}, u32[]{:S(2)}) copy-start(bf16[4,1,4,256,512]{4,3,2,1,0:T(8,128)(2,1)} %param.11) | copy-start | bytes 12582916
  14.8 2.2 %copy-start.2 = (s32[4]{0:T(128)S(1)}, s32[4]{0:T(128)}, u32[]{:S(2)}) copy-start(s32[4]{0:T(128)} %order.1) | copy-start | bytes 52
  23.0 0.7 copy-start.5
  23.0 0.7 copy-start.6
  23.0 16.8 %copy-start.3 = (s32[4]{0:T(128)S(1)}, s32[4]{0:T(128)}, u32[]{:S(2)}) copy-start(s32[4]{0:T(128)} %param.16) | copy-start | bytes 52
  23.1 98.4 %all-gather.7.cloned.1.call-start = ((), (), s32[]{:S(2)}) async-start(), calls=%async_computation.3 | async-start | bytes 4055040 | tf_op jit(solution)/shard_map/all_gather | solution.py:255
  58.6 136.1 %all-gather.5.cloned.1.call-start = ((), (), s32[]{:S(2)}) async-start(), calls=%async_computation.1 | async-start | bytes 5242880 | tf_op jit(solution)/shard_map/all_gather | solution.py:194
Sparse Core Ops, SparseCore 0:
  23.2 35.3 reduce-scatter.1
  62.1 59.3 all-gather.6
  123.5 51.3 all-gather.4

commit v3 on v2

--- a/solution.py
+++ b/solution.py
@@ -71,13 +71,18 @@
     batches = pl.num_programs(0)
     total = 4
     k_now = pl.program_id(0)
-    groups, mats, obs, width = p_ref.shape
+    lags, groups, mats, rows_in, width = p_ref.shape
+    obs = lags * rows_in
     members = groups * width
 
     @pl.when(k_now == 0)
     def _():
-        for g in range(groups):
-            ps[:, :, g * width : (g + 1) * width] = p_ref[g]
+        for piece in range(lags * mats):
+            mat, part = divmod(piece, lags)
+            for g in range(groups):
+                ps[mat, part * rows_in : (part + 1) * rows_in, g * width : (g + 1) * width] = (
+                    p_ref[piece // mats, g, piece % mats]
+                )
         ms[...] = m_ref[...]
 
     here = lax.shift_left(1, k_now) - 1
@@ -247,13 +252,14 @@
     errors = small_all[owner_row, mats + batches + batch_order]
 
     summed = lax.psum_scatter(
-        part.reshape(mats * obs, width), ("space", "lag"), scatter_dimension=0, tiled=True
+        part.reshape(mats * obs, width), ("lag", "space"), scatter_dimension=0, tiled=True
     )
     summed, values, errors, mean_sum = lax.optimization_barrier(
         (summed, values, errors, mean_sum)
     )
-    p_all = lax.all_gather(summed, ("member", "space", "lag"), axis=0, tiled=True)
-    p_all = p_all.reshape(groups, mats, obs, width)
+    p_half = lax.all_gather(summed, ("member", "space"), axis=0, tiled=True)
+    p_all = lax.all_gather(p_half, "lag", axis=0)
+    p_all = p_all.reshape(lags, groups, mats, obs // lags, width)
     own = lax.axis_index("member").astype(jnp.int32).reshape(1)
     mean_cols = jnp.pad(mean_sum[:, :, None], ((0, 0), (0, 0), (0, width - 1)))
 
@@ -264,7 +270,9 @@
             num_scalar_prefetch=1,
             grid=(batches,),
             in_specs=[
-                pl.BlockSpec((groups, mats, obs, width), lambda k, o: (0, 0, 0, 0)),
+                pl.BlockSpec(
+                    (lags, groups, mats, obs // lags, width), lambda k, o: (0, 0, 0, 0, 0)
+                ),
                 pl.BlockSpec((mats, obs, width), lambda k, o: (0, 0, 0)),
                 pl.BlockSpec((1, obs, 1), lambda k, o: (k, 0, 0)),
                 pl.BlockSpec((1, obs, 1), lambda k, o: (k, 0, 0)),

time: 210 us -> 226 us (1.076)
  waiting for transfers between devices: 75.4 us -> 91.3 us
    all_gather x1 -> x2, waiting for transfers between devices: 57.9 us -> 71.2 us  [the longest x1 62.3 us: body(): p_half = lax.all_gather(summed, ('member', 'space'), axis=0, tiled=True)]
    reduce_scatter x1, waiting for transfers between devices: 16.9 us -> 19.7 us  [body(): lax.psum_scatter(part.reshape(mats * obs, width), ('lag', 'space'), scatt...]
  transfers between devices with their start and end apart: 3 -> 4, of which waited for: 2 -> 3; matrix products, arithmetic and copies ran while one was open for 3% -> 3% of each run, Pallas kernels for 35% -> 32%
where the time goes in v3:
time: 226 us
  waiting for transfers between devices  91.3 us (40%)
  Pallas kernels  88.1 us (39%)
  blocking collectives  16.2 us (7%)
  between operations  13.9 us (6%)
  local copies, waits for them, and re-layouts  13.4 us (6%)
  other arithmetic  2.9 us (1%)
    pallas_call x1, Pallas kernels, body(): pl.pallas_call(chain_kernel, out_shape=jax.ShapeDtypeStruct((2 ** batches...  73.3 us
    all_gather x1, waiting for transfers between devices, body(): p_half = lax.all_gather(summed, ('member', 'space'), axis=0, tiled=True)  62.3 us
    reduce_scatter x1, waiting for transfers between devices, body(): lax.psum_scatter(part.reshape(mats * obs, width), ('lag', 'space'), scatt...  19.7 us
    all_gather x1, blocking collectives, body(): small_all = lax.all_gather(small, ('space', 'lag'), axis=0)  16.2 us
    all_gather x1, waiting for transfers between devices, body(): p_all = lax.all_gather(p_half, 'lag', axis=0)  8.81 us
    pallas_call x1, Pallas kernels, body(): pl.pallas_call(final_kernel, out_shape=(jax.ShapeDtypeStruct((tiles, tile...  8.7 us
    pallas_call x1, Pallas kernels, body(): pl.pallas_call(prints_kernel, out_shape=(jax.ShapeDtypeStruct((mats, obs,...  6.05 us
  transfers between devices with their start and end apart: 4, of which 3 were waited for; matrix products, arithmetic and copies ran while one was open for 3% of the time, Pallas kernels for 32%

profile of v3, /device:TPU:0, one launch (start us, length us, event | category | flops | bytes accessed | tf_op | source)
XLA Modules:
  0.0 226.1 jit_solution(4976317665125390907)
XLA Ops:
  7.2 0.0 copy-start
  7.2 0.0 copy-start.4
  7.2 0.0 reduce-scatter.2.cloned.1.call-start
  7.2 0.7 compare_select_fusion.5
  8.0 0.0 copy-done
  8.0 0.6 gather_fusion
  8.6 0.1 reshape.109.tiles
  8.7 1.3 gather_fusion.1
  9.9 0.1 iota_compare_fusion.2
  10.0 0.1 fusion.3
  10.1 0.1 lt.63
  10.2 0.1 broadcast_select_fusion
  10.3 0.6 select_subtract_fusion
  10.9 0.1 reshape.150
  11.0 0.1 add.75
  11.1 0.1 add.76
  11.1 0.8 convert_reduce_fusion
  11.9 2.1 convert_element_type.20
  14.0 0.7 gather_fusion.5
  14.7 0.0 copy-done.4
  14.7 0.0 copy-start.1
  14.7 0.0 copy-start.2
  14.7 0.5 fusion.1.x_ref
  15.2 1.7 copy-done.1
  16.9 0.0 copy-done.2
  16.9 6.0 %prints.1 = (bf16[15,256,128]{2,1,0:T(8,128)(2,1)}, f32[15,256,128]{2,1,0:T(8,128)S(1)}) custom-call(s32[4]{0:T(128)S(1)} %copy-done.2, s32[16]{0:T(128)S(1)} %reshape.109.tiles, s32[16]{0:T(128)S(1)} %fusion.14.dest, bf16[4,4,256,512]{3,2,1,0:T(8,128)(2,1)S(1)} %bitcast.40, bf16[8,512,256]{2,1,0:T(8,128)(2,1)S(1)} %fusion.1.x_ref), custom_call_target="tpu_custom_call" | custom-call | tf_op jit(solution)/shard_map/prints/pallas_call | solution.py:218
  23.0 0.0 copy-start.5
  23.0 0.0 copy-start.6
  23.0 0.0 copy-start.3
  23.0 0.0 reduce-scatter.2.cloned.1.call-update
  23.0 0.0 all-gather.9.cloned.1.call-start
  23.1 0.6 slice_reduce_fusion
  23.6 0.0 copy-done.5
  23.7 0.0 copy-done.6
  23.7 16.2 %all-gather.2 = f32[8,23,256]{2,1,0:T(8,128)S(1)} all-gather(f32[1,23,256]{2,1,0:T(8,128)S(1)} %maximum_bitcast_fusion), channel_id=2, replica_groups=mesh['space'=4,'member'=4,'lag'=2] {'space','lag'}, dimensions={0}, use_global_device_ids=true | all-gather | bytes 211968 | tf_op jit(solution)/shard_map/all_gather | solution.py:247
  39.9 0.1 copy.24
  39.9 0.0 copy-done.3
  40.0 0.6 gather_fusion.2
  40.6 0.6 gather_fusion.4
  41.2 0.6 gather_fusion.3
  41.8 19.7 %reduce-scatter.2.cloned.1.call-done = bf16[480,128]{1,0:T(8,128)(2,1)} async-done(((bf16[3840,128]{1,0:T(8,128)(2,1)}), bf16[480,128]{1,0:T(8,128)(2,1)}) %reduce-scatter.2.cloned.1.call-update) | async-done | bytes 122896 | tf_op jit(solution)/shard_map/reduce_scatter | solution.py:254
  61.5 0.0 all-gather.9.cloned.1.call-update
  61.5 0.0 all-gather.11.cloned.1.call-start
  61.6 62.3 %all-gather.9.cloned.1.call-done = bf16[7680,128]{1,0:T(8,128)(2,1)} async-done(((bf16[480,128]{1,0:T(8,128)(2,1)}), bf16[7680,128]{1,0:T(8,128)(2,1)}) %all-gather.9.cloned.1.call-update) | async-done | bytes 1966096 | tf_op jit(solution)/shard_map/all_gather | solution.py:260
  123.9 0.0 all-gather.11.cloned.1.call-update
  123.9 0.2 all-gather.7.cloned.1.call-start
  124.2 0.3 all-gather.7.cloned.1.call-update
  124.5 0.6 copy.26
  125.1 1.0 copy.27.val_ref
  126.2 1.0 copy.28.err_ref
  127.2 1.5 pad.9.m_ref
  128.7 8.8 %all-gather.11.cloned.1.call-done = bf16[15360,128]{1,0:T(8,128)(2,1)} async-done(((bf16[7680,128]{1,0:T(8,128)(2,1)}), bf16[15360,128]{1,0:T(8,128)(2,1)}) %all-gather.11.cloned.1.call-update) | async-done | bytes 3932176 | tf_op jit(solution)/shard_map/all_gather | solution.py:261
  137.5 73.3 %chain.1.c_ref = bf16[16,512,256]{2,1,0:T(8,128)(2,1)} custom-call(s32[1]{0:T(128)} %bitcast.4.own_ref, bf16[2,4,15,128,128]{4,3,2,1,0:T(8,128)(2,1)} %bitcast.50, f32[15,256,128]{2,1,0:T(8,128)} %pad.9.m_ref, f32[4,256,1]{2,1,0:T(8,128)} %copy.27.val_ref, f32[4,256,1]{2,1,0:T(8,128)} %copy.28.err_ref), custom_call_target="tpu_custom_call" | custom-call | flops 20000000000 | bytes 10000000 | tf_op jit(solution)/shard_map/chain/pallas_call | solution.py:266
  210.8 0.0 all-gather.7.cloned.1.call-done.all_ref
  210.8 8.7 %final.1 = (bf16[8,512,128]{2,1,0:T(8,128)(2,1)}, f32[8,1,512]{2,1,0:T(1,128)}) custom-call(s32[8]{0:T(128)} %get-tuple-element.21.history, bf16[8,512,128]{2,1,0:T(8,128)(2,1)} %bitcast.42, bf16[4,4096,128]{2,1,0:T(8,128)(2,1)} %all-gather.7.cloned.1.call-done.all_ref, f32[8,1,512]{2,1,0:T(1,128)} %bitcast.45, bf16[16,512,256]{2,1,0:T(8,128)(2,1)} %chain.1.c_ref), custom_call_target="tpu_custom_call" | custom-call | tf_op jit(solution)/shard_map/final/pallas_call | solution.py:299
  (9 shorter events, 0.1 us)
Async XLA Ops:
  7.2 0.8 copy-start
  7.2 7.6 %copy-start.4 = (bf16[1,4096,128]{2,1,0:T(8,128)(2,1)S(1)}, bf16[1,4096,128]{2,1,0:T(8,128)(2,1)}, u32[]{:S(2)}) copy-start(bf16[1,4096,128]{2,1,0:T(8,128)(2,1)} %param.9) | copy-start | bytes 3145732
  7.2 54.3 %reduce-scatter.2.cloned.1.call-start = ((), (), s32[]{:S(2)}) async-start(), calls=%async_computation.2 | async-start | bytes 1105920 | tf_op jit(solution)/shard_map/reduce_scatter | solution.py:254
  14.7 2.2 copy-start.1
  14.7 2.2 copy-start.2
  23.0 0.7 copy-start.5
  23.0 0.7 copy-start.6
  23.0 17.0 %copy-start.3 = (s32[4]{0:T(128)S(1)}, s32[4]{0:T(128)}, u32[]{:S(2)}) copy-start(s32[4]{0:T(128)} %param.16) | copy-start | bytes 52
  23.0 100.9 %all-gather.9.cloned.1.call-start = ((), (), s32[]{:S(2)}) async-start(), calls=%async_computation.3 | async-start | bytes 2088960 | tf_op jit(solution)/shard_map/all_gather | solution.py:260
  61.5 76.0 %all-gather.11.cloned.1.call-start = ((), (), s32[]{:S(2)}) async-start(), calls=%async_computation.4 | async-start | bytes 5898240 | tf_op jit(solution)/shard_map/all_gather | solution.py:261
  123.9 86.9 %all-gather.7.cloned.1.call-start = ((), (), s32[]{:S(2)}) async-start(), calls=%async_computation.1 | async-start | bytes 5242880 | tf_op jit(solution)/shard_map/all_gather | solution.py:199
Sparse Core Ops, SparseCore 0:
  23.1 38.3 reduce-scatter.1
  64.6 59.2 all-gather.8
  125.5 11.9 all-gather.10
  139.4 53.8 all-gather.6
